TPU v7x, 32 devices: a whole 2x2x4 slice. The times are simulated.
32 devices in a mesh: row: 8 (over y, x, core), col: 4 (over z).
Axes of the slice: x: 2, y: 2, z: 4, core: 2. Of those that a mesh axis runs over, the one named last changes fastest.
Arguments:
- slab: bfloat16 [2, 640, 640, 640], P(None, 'col', 'row'), may hold values from -6 to 6
- coef_virtual: bfloat16 [640, 576], replicated, may hold values from -0.25 to 0.25
- coef_occupied: bfloat16 [640, 64], replicated, may hold values from -0.25 to 0.25
- occ_level: int32 [64], replicated, may hold values from -160 to -16
- virt_level: int32 [576], replicated, may hold values from 16 to 192
- orbital_index: int32 [2], replicated, may hold values from 0 to 63
Outputs:
- back_slab: bfloat16 [2, 640, 640, 640], P(None, 'col', 'row')
All inputs are finite; a program needn't handle non-finite values.
Results may differ from a plain program's by a relative error of at most 0.008.
Values may be sent and summed in bfloat16 or wider, within the bound.
A program may use at most 256 MiB of HBM per device.

v0:
```python
import jax
import jax.numpy as jnp
from jax import lax
from jax.sharding import PartitionSpec as P

NB = 640
NO = 64
NV = 576


def local(slab, coef_virtual, coef_occupied, occ_level, virt_level, orbital_index):
    n_row = lax.axis_size("row")
    n_col = lax.axis_size("col")
    virt_local = NV // n_col
    basis_row = NB // n_row
    basis_col = NB // n_col
    eo = occ_level.astype(jnp.float32) / 64.0
    ev = virt_level.astype(jnp.float32) / 64.0
    picks = orbital_index[:, None] == jnp.arange(NO, dtype=jnp.int32)[None, :]
    energy_i = jnp.sum(jnp.where(picks, eo[None, :], jnp.float32(0.0)), axis=1)
    virt_start = lax.axis_index("col") * virt_local
    ev_part = lax.dynamic_slice_in_dim(ev, virt_start, virt_local, 0)
    occ_blocks = coef_occupied.reshape(n_col, basis_col, NO)
    virt_rows = coef_virtual.reshape(n_row, basis_row, NV)
    virt_cols = coef_virtual.T.reshape(n_col, virt_local, NB)
    basis_start = lax.axis_index("row") * basis_row
    coef_mine = lax.dynamic_slice_in_dim(coef_virtual, basis_start, basis_row, 0)
    results = []
    for orbit in range(slab.shape[0]):
        block = slab[orbit].reshape(basis_col * basis_row, NB)
        first = jnp.einsum(
            "na,xn->ax", coef_virtual, block, preferred_element_type=jnp.float32
        ).astype(jnp.bfloat16)
        first = lax.all_to_all(first, "col", split_axis=0, concat_axis=0, tiled=True)
        first = first.reshape(n_col, virt_local, basis_col, basis_row)
        second = jnp.einsum(
            "salm,slj->jam", first, occ_blocks, preferred_element_type=jnp.float32
        ).astype(jnp.bfloat16)
        whole = lax.all_gather(second, "row", axis=0, tiled=True)
        whole = whole.reshape(n_row, NO, virt_local, basis_row)
        third = jnp.einsum("rjam,rmb->jab", whole, virt_rows, preferred_element_type=jnp.float32)
        denom = ev[None, None, :] + ev_part[None, :, None] - energy_i[orbit] - eo[:, None, None]
        amplitude = (third / denom).astype(jnp.bfloat16)
        back_one = jnp.einsum(
            "jab,mb->mja", amplitude, coef_mine, preferred_element_type=jnp.float32
        ).astype(jnp.bfloat16)
        back_two = jnp.einsum(
            "mja,lj->lma", back_one, coef_occupied, preferred_element_type=jnp.float32
        ).astype(jnp.bfloat16)
        gathered = lax.all_to_all(back_two, "col", split_axis=0, concat_axis=0, tiled=True)
        gathered = gathered.reshape(n_col, basis_col, basis_row, virt_local)
        result = jnp.einsum(
            "slma,san->lmn", gathered, virt_cols, preferred_element_type=jnp.float32
        )
        results.append(result.astype(jnp.bfloat16))
    return jnp.stack(results, axis=0)


def solution(mesh):
    placed = (P(None, "col", "row", None), P(), P(), P(), P(), P())
    return jax.shard_map(
        local, mesh=mesh, in_specs=placed, out_specs=P(None, "col", "row", None), check_vma=False
    )
```

profile of v0, /device:TPU:0, one launch (start us, length us, event | category | flops | bytes accessed | tf_op | source)
XLA Modules:
  0.0 1988.1 jit_solution(5003275165701705367)
XLA Ops:
  6.5 0.0 copy-start
  6.5 22.7 %fusion.45 = (bf16[1,160,80,640]{3,2,1,0:T(8,128)(2,1)}, bf16[1,160,80,640]{3,2,1,0:T(8,128)(2,1)}) fusion(bf16[2,160,80,640]{3,2,1,0:T(8,128)(2,1)} %param.6), kind=kLoop, calls=%fused_computation.43 | loop fusion | bytes 65536000 | tf_op jit(solution)/shard_map/slice | solution.py:30
  29.3 0.0 copy-done
  29.3 20.4 %convolution_convert_fusion = bf16[576,12800]{1,0:T(8,128)(2,1)} fusion(bf16[640,576]{0,1:T(8,128)(2,1)S(1)} %copy-done, bf16[12800,640]{1,0:T(8,128)(2,1)} %bitcast.110), kind=kOutput, calls=%fused_computation.7 | convolution fusion | flops 9444556800 | bytes 31866880 | tf_op jit(solution)/shard_map/na,xn->ax/dot_general | solution.py:31
  49.7 6.7 all-to-all-start.2
  56.3 20.4 %convolution_convert_fusion.1 = bf16[576,12800]{1,0:T(8,128)(2,1)} fusion(bf16[640,576]{0,1:T(8,128)(2,1)S(1)} %copy-done, bf16[12800,640]{1,0:T(8,128)(2,1)} %bitcast.109), kind=kOutput, calls=%fused_computation.8 | convolution fusion | flops 9444556800 | bytes 31866880 | tf_op jit(solution)/shard_map/na,xn->ax/dot_general | solution.py:31
  76.8 0.0 copy-start.2
  76.8 300.7 %all-to-all-done.2 = bf16[4,144,12800]{2,1,0:T(8,128)(2,1)} async-done(((bf16[4,144,12800]{2,1,0:T(8,128)(2,1)}), bf16[4,144,12800]{2,1,0:T(8,128)(2,1)}, u32[]{:S(2)}, u32[]{:S(2)}) %all-to-all-start.2) | async-done | bytes 14745632 | tf_op jit(solution)/shard_map/all_to_all | solution.py:34
  377.5 6.7 all-to-all-start
  384.2 0.4 all-gather.5.cloned.1.call-start
  384.6 0.0 copy-done.2
  384.6 0.1 reshape.95
  384.8 45.0 %copy.73 = bf16[4,144,12800]{2,0,1:T(4,128)(2,1)} copy(bf16[4,144,12800]{2,1,0:T(8,128)(2,1)} %all-to-all-done.2) | data formatting | bytes 29491200 | tf_op jit(solution)/shard_map/all_to_all | solution.py:34
  429.8 37.6 %reshape.100 = bf16[4,144,160,80]{3,2,0,1:T(8,128)(2,1)} reshape(bf16[4,144,12800]{2,0,1:T(4,128)(2,1)} %copy.73) | data formatting | bytes 29491200 | tf_op jit(solution)/shard_map/reshape | solution.py:35
  467.4 0.0 copy-start.4
  467.4 0.0 copy-start.5
  467.4 0.0 copy-start.6
  467.4 13.5 fusion.21
  480.9 0.0 all-gather.5.cloned.1.call-update
  481.0 0.0 all-gather.3.cloned.1.call-start
  481.0 0.4 copy.64
  481.4 0.0 copy-done.4
  481.4 0.1 dynamic_slice.7
  481.5 0.0 copy-done.5
  481.5 0.0 copy-done.6
  481.5 0.2 fusion.42
  481.7 0.6 fusion.46
  482.3 2.1 add_subtract_fusion.1
  484.3 218.9 %all-to-all-done = bf16[4,144,12800]{2,1,0:T(8,128)(2,1)} async-done(((bf16[4,144,12800]{2,1,0:T(8,128)(2,1)}), bf16[4,144,12800]{2,1,0:T(8,128)(2,1)}, u32[]{:S(2)}, u32[]{:S(2)}) %all-to-all-start) | async-done | bytes 14745632 | tf_op jit(solution)/shard_map/all_to_all | solution.py:34
  703.2 45.1 %copy.65 = bf16[4,144,12800]{2,0,1:T(4,128)(2,1)} copy(bf16[4,144,12800]{2,1,0:T(8,128)(2,1)} %all-to-all-done) | data formatting | bytes 29491200 | tf_op jit(solution)/shard_map/all_to_all | solution.py:34
  748.3 37.6 %reshape.94 = bf16[4,144,160,80]{3,2,0,1:T(8,128)(2,1)} reshape(bf16[4,144,12800]{2,0,1:T(4,128)(2,1)} %copy.65) | data formatting | bytes 29491200 | tf_op jit(solution)/shard_map/reshape | solution.py:35
  785.9 13.5 fusion.20
  799.3 0.0 all-gather.3.cloned.1.call-update
  799.4 0.0 all-gather.5.cloned.1.call-done
  799.4 59.8 %fusion.22 = bf16[80,64,144]{0,2,1:T(8,128)(2,1)} fusion(f32[144,576]{1,0:T(8,128)S(1)} %get-tuple-element.8, f32[64]{0:T(128)S(1)} %convert_multiply_fusion.1, bf16[8,80,576,1]{2,1,0,3:T(8,128)(2,1)S(1)} %bitcast.115, bf16[8,64,144,80]{3,1,0,2:T(8,128)(2,1)} %bitcast.117, bf16[640,576]{1,0:T(8,128)(2,1)S(1)} %copy.64, s32[]{:T(128)S(6)} %select_n.10), kind=kOutput, calls=%fused_computation.23 | convolution fusion | flops 7660781568 | bytes 14561796 | tf_op jit(solution)/shard_map/jab,mb->mja/dot_general | solution.py:44
  859.2 5.0 copy.76
  864.1 7.6 convert_bitcast_fusion
  871.7 30.2 %copy.77 = bf16[640,80,144]{1,2,0:T(8,128)(2,1)} copy(bf16[640,80,144]{0,2,1:T(8,128)(2,1)} %convert_bitcast_fusion) | data formatting | bytes 29491200 | tf_op jit(solution)/shard_map/convert_element_type | solution.py:49
  902.0 0.0 copy-start.3
  902.0 8.3 all-to-all-start.3
  910.3 0.0 all-gather.3.cloned.1.call-done
  910.3 0.0 copy-done.3
  910.3 45.5 %fusion.27 = bf16[80,64,144]{0,2,1:T(8,128)(2,1)} fusion(f32[64]{0:T(128)S(1)} %convert_multiply_fusion.1, f32[144,576]{1,0:T(8,128)S(1)} %copy-done.3, bf16[8,80,576,1]{2,1,0,3:T(8,128)(2,1)S(1)} %bitcast.116, bf16[8,64,144,80]{3,1,0,2:T(8,128)(2,1)} %bitcast.118, bf16[640,576]{1,0:T(8,128)(2,1)S(1)} %copy.64, s32[]{:T(128)S(6)} %select_n.10), kind=kOutput, calls=%fused_computation.24 | convolution fusion | flops 7660781568 | bytes 14561796 | tf_op jit(solution)/shard_map/jab,mb->mja/dot_general | solution.py:44
  955.8 5.0 copy.69
  960.8 7.4 convert_bitcast_fusion.1
  968.2 30.3 %copy.70 = bf16[640,80,144]{1,2,0:T(8,128)(2,1)} copy(bf16[640,80,144]{0,2,1:T(8,128)(2,1)} %convert_bitcast_fusion.1) | data formatting | bytes 29491200 | tf_op jit(solution)/shard_map/convert_element_type | solution.py:49
  998.5 0.0 copy-start.1
  998.5 420.1 %all-to-all-done.3 = bf16[640,80,144]{1,2,0:T(8,128)(2,1)} async-done(((bf16[640,80,144]{1,2,0:T(8,128)(2,1)}), bf16[640,80,144]{1,2,0:T(8,128)(2,1)}, u32[]{:S(2)}, u32[]{:S(2)}) %all-to-all-start.3) | async-done | bytes 14745632 | tf_op jit(solution)/shard_map/all_to_all | solution.py:50
  1418.6 8.1 all-to-all-start.1
  1426.7 0.0 copy-done.1
  1426.8 23.4 %fusion.7 = bf16[1,160,80,640]{3,2,1,0:T(8,128)(2,1)} fusion(bf16[4,160,80,144]{2,3,1,0:T(8,128)(2,1)} %bitcast.34, bf16[4,144,640,1]{2,1,3,0:T(8,128)(2,1)S(1)} %bitcast.113), kind=kOutput, calls=%fused_computation.14 | convolution fusion | flops 9445376000 | bytes 31866880 | tf_op jit(solution)/shard_map/slma,san->lmn/dot_general | solution.py:52
  1450.2 485.0 %all-to-all-done.1 = bf16[640,80,144]{1,2,0:T(8,128)(2,1)} async-done(((bf16[640,80,144]{1,2,0:T(8,128)(2,1)}), bf16[640,80,144]{1,2,0:T(8,128)(2,1)}, u32[]{:S(2)}, u32[]{:S(2)}) %all-to-all-start.1) | async-done | bytes 14745632 | tf_op jit(solution)/shard_map/all_to_all | solution.py:50
  1935.1 23.5 %fusion.6 = bf16[1,160,80,640]{3,2,1,0:T(8,128)(2,1)} fusion(bf16[4,160,80,144]{2,3,1,0:T(8,128)(2,1)} %bitcast.15, bf16[4,144,640,1]{2,1,3,0:T(8,128)(2,1)S(1)} %bitcast.114), kind=kOutput, calls=%fused_computation.13 | convolution fusion | flops 9445376000 | bytes 31866880 | tf_op jit(solution)/shard_map/slma,san->lmn/dot_general | solution.py:52
  1958.6 22.4 %pad_maximum_fusion = bf16[2,160,80,640]{3,2,1,0:T(8,128)(2,1)} fusion(bf16[1,160,80,640]{3,2,1,0:T(8,128)(2,1)} %fusion.7, bf16[1,160,80,640]{3,2,1,0:T(8,128)(2,1)} %fusion.6), kind=kLoop, calls=%fused_computation.2 | loop fusion | flops 16384000 | bytes 65536000 | tf_op jit(solution)/shard_map/stack | solution.py:56
  (2 shorter events, 0.0 us)
Async XLA Ops:
  6.5 22.7 %copy-start = (bf16[640,576]{0,1:T(8,128)(2,1)S(1)}, bf16[640,576]{0,1:T(8,128)(2,1)}, u32[]{:S(2)}) copy-start(bf16[640,576]{0,1:T(8,128)(2,1)} %param.7) | copy-start | bytes 2211844
  49.7 327.8 %all-to-all-start.2 = ((bf16[4,144,12800]{2,1,0:T(8,128)(2,1)}), bf16[4,144,12800]{2,1,0:T(8,128)(2,1)}, u32[]{:S(2)}, u32[]{:S(2)}) async-start(bf16[4,144,12800]{2,1,0:T(8,128)(2,1)} %bitcast.112), calls=%async_computation.2 | async-start | bytes 29491200 | tf_op jit(solution)/shard_map/all_to_all | solution.py:34
  76.8 307.9 %copy-start.2 = (bf16[640,64]{0,1:T(8,128)(2,1)S(1)}, bf16[640,64]{0,1:T(8,128)(2,1)}, u32[]{:S(2)}) copy-start(bf16[640,64]{0,1:T(8,128)(2,1)} %param.8) | copy-start | bytes 245764
  377.5 325.7 %all-to-all-start = ((bf16[4,144,12800]{2,1,0:T(8,128)(2,1)}), bf16[4,144,12800]{2,1,0:T(8,128)(2,1)}, u32[]{:S(2)}, u32[]{:S(2)}) async-start(bf16[4,144,12800]{2,1,0:T(8,128)(2,1)} %bitcast.111), calls=%async_computation | async-start | bytes 29491200 | tf_op jit(solution)/shard_map/all_to_all | solution.py:34
  384.2 415.2 %all-gather.5.cloned.1.call-start = ((), (), s32[]{:S(2)}) async-start(), calls=%async_computation.5 | async-start | bytes 21233664 | tf_op jit(solution)/shard_map/all_gather | solution.py:39
  467.4 14.0 copy-start.4
  467.4 14.1 copy-start.5
  467.4 14.1 copy-start.6
  481.0 429.3 %all-gather.3.cloned.1.call-start = ((), (), s32[]{:S(2)}) async-start(), calls=%async_computation.4 | async-start | bytes 21233664 | tf_op jit(solution)/shard_map/all_gather | solution.py:39
  902.0 8.3 copy-start.3
  902.0 516.6 %all-to-all-start.3 = ((bf16[640,80,144]{1,2,0:T(8,128)(2,1)}), bf16[640,80,144]{1,2,0:T(8,128)(2,1)}, u32[]{:S(2)}, u32[]{:S(2)}) async-start(bf16[640,80,144]{1,2,0:T(8,128)(2,1)} %copy.77), calls=%async_computation.3 | async-start | bytes 47185920 | tf_op jit(solution)/shard_map/all_to_all | solution.py:50
  998.5 428.3 %copy-start.1 = (bf16[640,576]{0,1:T(8,128)(2,1)S(1)}, bf16[640,576]{0,1:T(8,128)(2,1)}, u32[]{:S(2)}) copy-start(bf16[640,576]{0,1:T(8,128)(2,1)} %param.7) | copy-start | bytes 2211844
  1418.6 516.5 %all-to-all-start.1 = ((bf16[640,80,144]{1,2,0:T(8,128)(2,1)}), bf16[640,80,144]{1,2,0:T(8,128)(2,1)}, u32[]{:S(2)}, u32[]{:S(2)}) async-start(bf16[640,80,144]{1,2,0:T(8,128)(2,1)} %copy.70), calls=%async_computation.1 | async-start | bytes 47185920 | tf_op jit(solution)/shard_map/all_to_all | solution.py:50
Sparse Core Ops, SparseCore 0:
  481.1 100.1 all-gather.4
  799.5 97.6 all-gather.2
where the time goes:
time: 2000 us; the launch traced here: 1990 us
  waiting for transfers between devices  1420 us (71%)
  local copies, waits for them, and re-layouts  260 us (13%)
  matrix products  235 us (12%)
  starting transfers between devices  30.3 us (2%)
  other arithmetic  24.7 us (1%)
    all_to_all x2, waiting for transfers between devices, local(): lax.all_to_all(back_two, 'col', split_axis=0, concat_axis=0, tiled=True)  905 us
    all_to_all x2, waiting for transfers between devices, local(): lax.all_to_all(first, 'col', split_axis=0, concat_axis=0, tiled=True)  520 us
    dot_general x2, matrix products, local(): jnp.einsum('jab,mb->mja', amplitude, coef_mine, preferred_element_type=jn...  105 us
    all_to_all x2, local copies, waits for them, and re-layouts, local(): lax.all_to_all(first, 'col', split_axis=0, concat_axis=0, tiled=True)  90.1 us
    reshape x2, local copies, waits for them, and re-layouts, local(): first = first.reshape(n_col, virt_local, basis_col, basis_row)  75.2 us
    convert_element_type x2, local copies, waits for them, and re-layouts, local(): back_two = jnp.einsum('mja,lj->lma', back_one, coef_occupied, preferred_e...  60.5 us
    dot_general x2, matrix products, local(): jnp.einsum('slma,san->lmn', gathered, virt_cols, preferred_element_type=j...  46.9 us
    dot_general x2, matrix products, local(): jnp.einsum('na,xn->ax', coef_virtual, block, preferred_element_type=jnp.f...  40.8 us
  transfers between devices with their start and end apart: 6, of which 4 were waited for; matrix products, arithmetic and copies ran while one was open for 22% of the time, Pallas kernels for 0%

commit v1 on v0

v1 whole, which is shorter than its diff:
```python
import functools

import jax
import jax.numpy as jnp
from jax import lax
from jax.experimental import pallas as pl
from jax.experimental.pallas import tpu as pltpu
from jax.sharding import PartitionSpec as P

MESH = pl.DeviceIdType.MESH
LAG = 2


def greet(n_row, n_col, row, col):
    barrier = pltpu.get_barrier_semaphore()

    def hello(step, carry):
        other = lax.rem(row + step, n_row)
        pl.semaphore_signal(barrier, inc=1, device_id=(other, col), device_id_type=MESH)
        return carry

    lax.fori_loop(1, n_row, hello, 0)

    @pl.when(col > 0)
    def _():
        pl.semaphore_signal(barrier, inc=1, device_id=(row, col - 1), device_id_type=MESH)

    @pl.when(col < n_col - 1)
    def _():
        pl.semaphore_signal(barrier, inc=1, device_id=(row, col + 1), device_id_type=MESH)

    beside = jnp.where(col > 0, 1, 0) + jnp.where(col < n_col - 1, 1, 0)
    pl.semaphore_wait(barrier, n_row - 1 + beside)


def exchange(n_row, n_col, part, cv, cvt, ev_down, ev_across, shift, out, recv, whole, ready,
             in_line_send, in_line_recv, in_row_send, in_row_recv, in_own,
             out_line_send, out_line_recv, out_row_send, out_row_recv, out_own):
    row, col = lax.axis_index("row"), lax.axis_index("col")
    last = n_col - 1
    orbits, _, _, subs, width, basis_row, nb = part.shape
    per_orbit = n_row * subs
    chunks = orbits * per_orbit
    units = subs * width
    at_end = (col == 0) | (col == last)
    greet(n_row, n_col, row, col)

    def split(i):
        return i // per_orbit, lax.rem(i, per_orbit) // subs, lax.rem(i, subs)


    def in_target(i):
        return lax.rem(row + 1 + split(i)[1], n_row)

    def in_line(half, i, source):
        ahead = col + 1 if half == 0 else col - 1
        return pltpu.make_async_remote_copy(
            src_ref=source, dst_ref=recv.at[half, i],
            send_sem=in_line_send.at[half, i], recv_sem=in_line_recv.at[half, i],
            device_id=(row, ahead), device_id_type=MESH)

    def in_row(half, i):
        orbit, _, sub = split(i)
        return pltpu.make_async_remote_copy(
            src_ref=recv.at[half, i], dst_ref=whole.at[orbit, row, sub],
            send_sem=in_row_send.at[i], recv_sem=in_row_recv.at[orbit, row, sub],
            device_id=(in_target(i), col), device_id_type=MESH)

    def in_own_copy(half, i):
        orbit, _, sub = split(i)
        return pltpu.make_async_copy(
            recv.at[half, i], whole.at[orbit, row, sub], in_own.at[orbit, sub])

    def in_work(half, place, i):
        orbit, _, sub = split(i)
        target = in_target(i)

        @pl.when(place == 0)
        def _():
            in_line(half, i, part.at[orbit, half, target, sub]).start()

        @pl.when(place > 0)
        def _():
            in_line(half, i, recv.at[half, i]).wait_recv()
            mine = part[orbit, half, target, sub].astype(jnp.float32)
            recv[half, i] = (recv[half, i].astype(jnp.float32) + mine).astype(recv.dtype)

        @pl.when((place > 0) & (place < last))
        def _():
            in_line(half, i, recv.at[half, i]).start()

        @pl.when((place == last) & (target != row))
        def _():
            in_row(half, i).start()

        @pl.when((place == last) & (target == row))
        def _():
            in_own_copy(half, i).start()


    def arrived(orbit):
        def one(k, carry):
            source, sub = k // subs, lax.rem(k, subs)

            @pl.when(source != row)
            def _():
                pltpu.make_async_remote_copy(
                    src_ref=recv.at[0, 0], dst_ref=whole.at[orbit, source, sub],
                    send_sem=in_row_send.at[0], recv_sem=in_row_recv.at[orbit, source, sub],
                    device_id=(source, col), device_id_type=MESH).wait_recv()

            @pl.when(source == row)
            def _():
                pltpu.make_async_copy(
                    recv.at[0, 0], whole.at[orbit, source, sub], in_own.at[orbit, sub]).wait()
            return carry

        lax.fori_loop(0, per_orbit, one, 0)

    def dot(a, b):
        return jnp.dot(a, b, preferred_element_type=jnp.float32)

    def middle(orbit, k):
        sub, j = k // width, lax.rem(k, width)
        x = whole[orbit, :, sub, j]
        if basis_row % 16 == 0:
            x = x.reshape(n_row * basis_row, nb)
        else:
            x = x.astype(jnp.float32).reshape(n_row * basis_row, nb).astype(whole.dtype)
        second = dot(x, cv[...]).astype(whole.dtype)
        third = dot(cvt[...], second)
        denom = ev_down[...] + ev_across[...] - shift[orbit, k]
        amplitude = (third / denom).astype(whole.dtype)
        back_one = dot(cv[...], amplitude).astype(whole.dtype)
        back = dot(back_one, cvt[...]).reshape(n_row, basis_row, nb)
        ready[orbit, :, sub, j] = back.astype(ready.dtype)

    def middle_at(orbit, k):
        @pl.when(at_end & (k == 0))
        def _():
            arrived(orbit)

        @pl.when(at_end & (k >= 0) & (k < units))
        def _():
            middle(orbit, k)


    def out_source(i):
        return lax.rem(row - split(i)[1] + n_row, n_row)

    def out_target(i):
        return lax.rem(row + split(i)[1], n_row)

    def out_line(half, i):
        ahead = col - 1 if half == 0 else col + 1
        orbit, _, sub = split(i)
        block = out.at[orbit, half, out_source(i), sub]
        return pltpu.make_async_remote_copy(
            src_ref=block, dst_ref=block,
            send_sem=out_line_send.at[half, i], recv_sem=out_line_recv.at[half, i],
            device_id=(row, ahead), device_id_type=MESH)

    def out_row(half, i):
        orbit, _, sub = split(i)
        target = out_target(i)
        return pltpu.make_async_remote_copy(
            src_ref=ready.at[orbit, target, sub], dst_ref=out.at[orbit, half, row, sub],
            send_sem=out_row_send.at[i], recv_sem=out_row_recv.at[i],
            device_id=(target, col), device_id_type=MESH)

    def out_own_copy(half, i):
        orbit, _, sub = split(i)
        return pltpu.make_async_copy(
            ready.at[orbit, row, sub], out.at[orbit, half, row, sub], out_own.at[orbit, sub])

    def give(half, i):
        @pl.when(split(i)[1] == 0)
        def _():
            out_own_copy(half, i).start()

        @pl.when(split(i)[1] != 0)
        def _():
            out_row(half, i).start()

    def take(half, i):
        orbit, _, sub = split(i)

        @pl.when(split(i)[1] == 0)
        def _():
            out_own_copy(half, i).wait()

        @pl.when(split(i)[1] != 0)
        def _():
            pltpu.make_async_remote_copy(
                src_ref=ready.at[orbit, row, sub], dst_ref=out.at[orbit, half, out_source(i), sub],
                send_sem=out_row_send.at[i], recv_sem=out_row_recv.at[i],
                device_id=(out_source(i), col), device_id_type=MESH).wait_recv()


    def in_step(s, carry):
        for half in (0, 1):
            place = col if half == 0 else last - col
            i = s - LAG * place

            @pl.when((i >= 0) & (i < chunks))
            def _():
                in_work(half, place, i)
        for orbit in range(orbits - 1):
            middle_at(orbit, s - ((orbit + 1) * per_orbit + LAG * last + 2))
        return carry

    lax.fori_loop(0, chunks + LAG * last, in_step, 0)

    first = max(1, min(6, per_orbit - units - 1))

    def open_(i, carry):
        for half in (0, 1):
            place = last - col if half == 0 else col

            @pl.when(place == 0)
            def _():
                give(half, i)
        return carry

    lax.fori_loop(0, first, open_, 0)

    def out_step(s, carry):
        for half in (0, 1):
            place = last - col if half == 0 else col
            i = s - LAG * place

            @pl.when((place == 0) & (i + first < chunks))
            def _():
                give(half, i + first)

            @pl.when((place == 0) & (i < chunks))
            def _():
                take(half, i)

            @pl.when((place > 0) & (i >= 0) & (i < chunks))
            def _():
                out_line(half, i).wait_recv()

            @pl.when((place < last) & (i >= 0) & (i < chunks))
            def _():
                out_line(half, i).start()
        middle_at(orbits - 1, s - 1)
        return carry

    lax.fori_loop(0, chunks + LAG * last, out_step, 0)

    def drain(i, carry):
        for half in (0, 1):
            place = col if half == 0 else last - col

            @pl.when(place < last)
            def _():
                in_line(half, i, recv.at[half, i]).wait_send()

            @pl.when((place == last) & (in_target(i) != row))
            def _():
                in_row(half, i).wait_send()

            @pl.when(place > 0)
            def _():
                out_line(half, i).wait_send()

            @pl.when((place == last) & (split(i)[1] != 0))
            def _():
                out_row(half, i).wait_send()
        return carry

    lax.fori_loop(0, chunks, drain, 0)


def run_exchange(n_row, n_col, part, cv, ev, shift):
    orbits, _, _, subs = part.shape[:4]
    block = part.shape[4:]
    chunks = orbits * n_row * subs
    dma = pltpu.SemaphoreType.DMA
    vmem = pl.BlockSpec(memory_space=pltpu.VMEM)
    held = (orbits, n_row, subs) + block
    return pl.pallas_call(
        functools.partial(exchange, n_row, n_col),
        out_shape=jax.ShapeDtypeStruct(part.shape, part.dtype),
        in_specs=[vmem] * 5 + [pl.BlockSpec(memory_space=pltpu.SMEM)],
        out_specs=pl.BlockSpec(memory_space=pl.ANY),
        scratch_shapes=[
            pltpu.VMEM((2, chunks) + block, part.dtype),
            pltpu.VMEM(held, part.dtype), pltpu.VMEM(held, part.dtype),
            dma((2, chunks)), dma((2, chunks)), dma((chunks,)), dma((orbits, n_row, subs)), dma((orbits, subs)),
            dma((2, chunks)), dma((2, chunks)), dma((chunks,)), dma((chunks,)), dma((orbits, subs)),
        ],
        compiler_params=pltpu.CompilerParams(
            collective_id=0, has_side_effects=True, vmem_limit_bytes=58 * 1024 * 1024),
        name="exchange",
    )(part, cv, cv.T, ev[:, None], ev[None, :], shift)


def local(slab, coef_virtual, coef_occupied, occ_level, virt_level, orbital_index):
    n_row = lax.axis_size("row")
    n_col = lax.axis_size("col")
    orbits, basis_col, basis_row, nb = slab.shape
    no = coef_occupied.shape[1]
    eo = occ_level.astype(jnp.float32) / 64.0
    ev = virt_level.astype(jnp.float32) / 64.0
    picks = orbital_index[:, None] == jnp.arange(no, dtype=jnp.int32)[None, :]
    energy_i = jnp.sum(jnp.where(picks, eo[None, :], jnp.float32(0.0)), axis=1)
    col = lax.axis_index("col")
    row = lax.axis_index("row")
    occ_mine = lax.dynamic_slice_in_dim(coef_occupied, col * basis_col, basis_col, 0)
    j_mine = no // (2 * n_row)
    subs = 2 if j_mine % 2 == 0 else 1
    j_start = jnp.where(col == 0, no // 2, 0) + row * j_mine
    eo_mine = lax.dynamic_slice_in_dim(eo, j_start, j_mine, 0)

    part = jnp.einsum(
        "lj,olmn->ojmn", occ_mine, slab, preferred_element_type=jnp.float32
    ).astype(jnp.bfloat16)
    part = part.reshape(orbits, 2, n_row, subs, j_mine // subs, basis_row, nb)
    shift = energy_i[:, None] + eo_mine[None, :]
    back = run_exchange(n_row, n_col, part, coef_virtual, ev, shift)
    back = back.reshape(orbits, no, basis_row, nb)
    return jnp.einsum(
        "lj,ojmn->olmn", occ_mine, back, preferred_element_type=jnp.float32
    ).astype(jnp.bfloat16)


def solution(mesh):
    placed = (P(None, "col", "row", None), P(), P(), P(), P(), P())
    return jax.shard_map(
        local, mesh=mesh, in_specs=placed, out_specs=P(None, "col", "row", None), check_vma=False
    )
```

time: 2000 us -> 431 us (0.22)
  waiting for transfers between devices: 1420 us -> 0 us
  Pallas kernels: 0 us -> 325 us
  local copies, waits for them, and re-layouts: 260 us -> 59.5 us
  matrix products: 235 us -> 43.5 us
  starting transfers between devices: 30.3 us -> 0 us
  other arithmetic: 24.7 us -> 2.87 us
    all_to_all x4 -> x0, waiting for transfers between devices: 1420 us -> none  [the longest x2 905 us: local(): lax.all_to_all(back_two, 'col', split_axis=0, concat_axis=0, tiled=True)]
    pallas_call x0 -> x1, Pallas kernels: none -> 325 us  [run_exchange(): pl.pallas_call(functools.partial(exchange, n_row, n_col), out_shape=jax.S...]
    dot_general x10 -> x2, matrix products: 235 us -> 43.5 us  [the longest x1 23.5 us: local(): jnp.einsum('lj,olmn->ojmn', occ_mine, slab, preferred_element_type=jnp.fl...]
    all_to_all x2 -> x0, local copies, waits for them, and re-layouts: 90.1 us -> none  [local(): lax.all_to_all(first, 'col', split_axis=0, concat_axis=0, tiled=True)]
    reshape x3 -> x0, local copies, waits for them, and re-layouts: 75.4 us -> none  [the longest x2 75.2 us: local(): first = first.reshape(n_col, virt_local, basis_col, basis_row)]
    all_to_all x4 -> x0, starting transfers between devices: 29.8 us -> none  [the longest x2 16.4 us: local(): lax.all_to_all(back_two, 'col', split_axis=0, concat_axis=0, tiled=True)]
    slice x2 -> x0, local copies, waits for them, and re-layouts: 23.3 us -> none  [the longest x1 22.7 us: local(): block = slab[orbit].reshape(basis_col * basis_row, NB)]
    another operation x1 -> x0, other arithmetic: 22.4 us -> none  [local(): return jnp.stack(results, axis=0)]
  transfers between devices with their start and end apart: 6 -> 0, of which waited for: 4 -> 0; matrix products, arithmetic and copies ran while one was open for 22% -> 0% of each run, Pallas kernels for 0% -> 0%
where the time goes in v1:
time: 431 us
  Pallas kernels  325 us (75%)
  local copies, waits for them, and re-layouts  59.5 us (14%)
  matrix products  43.5 us (10%)
    pallas_call x1, Pallas kernels, run_exchange(): pl.pallas_call(functools.partial(exchange, n_row, n_col), out_shape=jax.S...  325 us
    convert_element_type x1, local copies, waits for them, and re-layouts, local(): return jnp.einsum('lj,ojmn->olmn', occ_mine, back, preferred_element_type...  34.4 us
    dot_general x1, matrix products, local(): jnp.einsum('lj,olmn->ojmn', occ_mine, slab, preferred_element_type=jnp.fl...  23.5 us
    convert_element_type x1, local copies, waits for them, and re-layouts, local(): part = jnp.einsum('lj,olmn->ojmn', occ_mine, slab, preferred_element_type...  21.3 us
    dot_general x1, matrix products, local(): jnp.einsum('lj,ojmn->olmn', occ_mine, back, preferred_element_type=jnp.fl...  20 us

profile of v1, /device:TPU:0, one launch (start us, length us, event | category | flops | bytes accessed | tf_op | source)
XLA Modules:
  0.0 430.8 jit_solution(18128364552134582302)
XLA Ops:
  0.0 0.0 copy-start
  0.0 0.7 convert_multiply_fusion.1
  0.7 0.1 dynamic_slice.7
  0.8 0.8 fusion.13
  1.6 0.7 broadcast_add_fusion.shift
  2.3 0.7 convert_multiply_fusion
  3.0 0.6 broadcast_in_dim.24.ev_across
  3.5 0.8 broadcast_in_dim.27.ev_down
  4.4 2.3 copy.20.cv
  6.7 0.0 copy-done
  6.7 23.5 %fusion.6 = bf16[2,64,80,640]{3,1,2,0:T(8,128)(2,1)S(1)} fusion(bf16[2,160,80,640]{3,2,1,0:T(8,128)(2,1)} %param.6, bf16[640,64]{0,1:T(8,128)(2,1)S(1)} %copy-done, s32[]{:T(128)S(6)} %select_n.14), kind=kOutput, calls=%fused_computation.5 | convolution fusion | flops 2103705600 | bytes 45907972 | tf_op jit(solution)/shard_map/lj,olmn->ojmn/dot_general | solution.py:317
  30.2 21.3 %copy.19 = bf16[2,64,80,640]{3,2,1,0:T(8,128)(2,1)} copy(bf16[2,64,80,640]{3,1,2,0:T(8,128)(2,1)S(1)} %fusion.6) | data formatting | bytes 26214400 | tf_op jit(solution)/shard_map/convert_element_type | solution.py:319
  51.5 324.9 %exchange.1 = bf16[2,2,8,2,2,80,640]{6,5,4,3,2,1,0:T(8,128)(2,1)} custom-call(bf16[2,2,8,2,2,80,640]{6,5,4,3,2,1,0:T(8,128)(2,1)} %bitcast.15, bf16[640,576]{1,0:T(8,128)(2,1)} %copy.20.cv, bf16[576,640]{1,0:T(8,128)(2,1)} %bitcast.16, f32[576,1]{1,0:T(8,128)} %broadcast_in_dim.27.ev_down, f32[1,576]{1,0:T(1,128)} %broadcast_in_dim.24.ev_across, ...), custom_call_target="tpu_custom_call" | custom-call | tf_op jit(solution)/shard_map/exchange/pallas_call | solution.py:283
  376.4 20.0 %convert_bitcast_fusion = bf16[2,160,80,640]{3,1,2,0:T(8,128)(2,1)} fusion(bf16[2,64,80,640]{3,2,1,0:T(8,128)(2,1)} %bitcast.14, bf16[640,64]{0,1:T(8,128)(2,1)S(1)} %copy-done, s32[]{:T(128)S(6)} %select_n.14), kind=kOutput, calls=%fused_computation.2 | convolution fusion | flops 2113536000 | bytes 45907972 | tf_op jit(solution)/shard_map/lj,ojmn->olmn/dot_general | solution.py:324
  396.4 34.4 %copy.23 = bf16[2,160,80,640]{3,2,1,0:T(8,128)(2,1)} copy(bf16[2,160,80,640]{3,1,2,0:T(8,128)(2,1)} %convert_bitcast_fusion) | data formatting | bytes 65536000 | tf_op jit(solution)/shard_map/convert_element_type | solution.py:326
Async XLA Ops:
  0.0 6.7 %copy-start = (bf16[640,64]{0,1:T(8,128)(2,1)S(1)}, bf16[640,64]{0,1:T(8,128)(2,1)}, u32[]{:S(2)}) copy-start(bf16[640,64]{0,1:T(8,128)(2,1)} %param.8) | copy-start | bytes 245764
